TPU v7x, 256 devices: a whole 4x4x8 slice. The times are simulated.
256 devices in a mesh: plane: 128 (over x, y, z), rad: 2 (over core).
Axes of the slice: x: 4, y: 4, z: 8, core: 2. Of those that a mesh axis runs over, the one named last changes fastest.
Arguments:
- coefficients: float32 [3, 128, 768, 256], P(None, 'plane', None, 'rad'), may hold values from -18 to 18
Outputs:
- convection: float32 [3, 128, 768, 256], P(None, 'plane', None, 'rad')
- stress: bfloat16 [6, 128, 768, 256], P(None, 'plane', None, 'rad')
All inputs are finite; a program needn't handle non-finite values.
Results may differ from a plain program's by a relative error of at most 0.0033.
Values sent between devices are 32-bit elements; how exact they have to be, the bound alone decides.
A program may use at most 128 MiB of HBM per device.

v0:
```python
import jax
import jax.numpy as jnp
from jax import lax
from jax.sharding import PartitionSpec as P

NZ = 128
NT = 768
NR = 256


inner_radius = 1.0
outer_radius = 1.4
axial_factor = 3.0
step_time = 0.002
component_pairs = ((0, 0), (1, 1), (2, 2), (0, 1), (0, 2), (1, 2))
pair_weights = (1.0, 1.0, 1.0, 2.0, 2.0, 2.0)


def chebyshev_tables(points):
    middle = 0.5 * (inner_radius + outer_radius)
    half_gap = 0.5 * (outer_radius - inner_radius)
    degree = jnp.arange(points, dtype=jnp.int32)
    phases = jnp.mod(degree[:, None] * degree[None, :], 2 * (points - 1))
    angles = jnp.pi * phases.astype(jnp.float32) / (points - 1)
    values = jnp.cos(angles)
    node_angles = jnp.pi * degree.astype(jnp.float32) / (points - 1)
    node_sines = jnp.sin(node_angles)
    inside = (degree > 0) & (degree < points - 1)
    safe_sines = jnp.where(inside, node_sines, 1.0)
    degree_real = degree.astype(jnp.float32)[:, None]
    squares = degree_real * degree_real
    parity = jnp.where(jnp.mod(degree, 2) == 0, -1.0, 1.0)[:, None]
    edges = jnp.where(degree[None, :] == 0, squares, parity * squares)
    slopes = (
        jnp.where(inside[None, :], degree_real * jnp.sin(angles) / safe_sines[None, :], edges)
        / half_gap
    )
    radius = middle + half_gap * jnp.cos(node_angles)
    return (values, slopes, radius)


def fourier_tables(points, keep, factor):
    indices = jnp.arange(points, dtype=jnp.int32)
    offset = indices[:, None] - indices[None, :]
    wrapped = jnp.mod(offset, 2 * points)
    turned = jnp.pi * wrapped.astype(jnp.float32) / points
    diagonal = offset == 0
    denominator = jnp.where(diagonal, 1.0, jnp.sin(turned))
    parity = jnp.where(jnp.mod(offset, 2) == 0, 0.5, -0.5)
    slopes = jnp.where(diagonal, 0.0, factor * parity * jnp.cos(turned) / denominator)
    window = jnp.pi * jnp.mod((2 * keep - 1) * offset, 2 * points).astype(jnp.float32) / points
    smooth = jnp.where(diagonal, (2 * keep - 1) / points, jnp.sin(window) / (points * denominator))
    return (slopes, smooth)


def across_theta(fields, matrix):
    return jnp.einsum("jk,fzkr->fzjr", matrix, fields, precision=lax.Precision.HIGHEST)


def along_axis(fields, matrix):
    return jnp.einsum("zy,fyab->fzab", matrix, fields, precision=lax.Precision.HIGHEST)


def pair_products(velocity):
    return jnp.stack([velocity[couple[0]] * velocity[couple[1]] for couple in component_pairs])


def strain_rate(velocity, radial, angular, axial, radius):
    inverse = 1.0 / radius
    strain = jnp.stack(
        [
            radial[0],
            angular[1] * inverse + velocity[0] * inverse,
            axial[2],
            0.5 * (radial[1] - velocity[1] * inverse + angular[0] * inverse),
            0.5 * (axial[0] + radial[2]),
            0.5 * (axial[1] + angular[2] * inverse),
        ]
    )
    weights = jnp.asarray(pair_weights, dtype=jnp.float32).reshape(6, 1, 1, 1)
    magnitude = jnp.sqrt(2.0 * jnp.sum(weights * strain * strain, axis=0))
    return (strain, magnitude)


def advection(velocity, radial, angular, axial, radius):
    inverse = 1.0 / radius
    carried = velocity[1] * inverse
    radial_part = (
        velocity[0] * radial[0]
        + carried * angular[0]
        + velocity[2] * axial[0]
        - velocity[1] * carried
    )
    swirl_part = (
        velocity[0] * radial[1]
        + carried * angular[1]
        + velocity[2] * axial[1]
        + velocity[0] * carried
    )
    axial_part = velocity[0] * radial[2] + carried * angular[2] + velocity[2] * axial[2]
    return jnp.stack([radial_part, swirl_part, axial_part])


def shell_terms(filtered):
    mean_velocity = filtered[0:3]
    mean_products = filtered[3:9]
    mean_strain = filtered[9:15]
    mean_scaled = filtered[15:21]
    weights = jnp.asarray(pair_weights, dtype=jnp.float32).reshape(6, 1, 1, 1)
    leonard = mean_products - pair_products(mean_velocity)
    mean_magnitude = jnp.sqrt(2.0 * jnp.sum(weights * mean_strain * mean_strain, axis=0))
    model = 2.0 * (mean_scaled - 4.0 * mean_magnitude[None] * mean_strain)
    cross_sum = jnp.sum(weights * leonard * model, axis=(0, 1, 2))
    model_sum = jnp.sum(weights * model * model, axis=(0, 1, 2))
    return (cross_sum, model_sum)


def shards(coefficients):
    local_radii = NR // lax.axis_size("rad")
    first_row = lax.axis_index("rad") * local_radii
    values, slopes, radius = chebyshev_tables(NR)
    own_values = lax.dynamic_slice_in_dim(values, first_row, local_radii, 1)
    own_slopes = lax.dynamic_slice_in_dim(slopes, first_row, local_radii, 1)
    own_radius = lax.dynamic_slice_in_dim(radius, first_row, local_radii, 0)
    pieces = lax.all_gather(coefficients, "rad", axis=3, tiled=True)
    velocity = jnp.einsum("cztk,kj->cztj", pieces, own_values, precision=lax.Precision.HIGHEST)
    radial = jnp.einsum("cztk,kj->cztj", pieces, own_slopes, precision=lax.Precision.HIGHEST)
    angle_slopes, angle_smooth = fourier_tables(NT, NT // 4, 1.0)
    axis_slopes, axis_smooth = fourier_tables(NZ, NZ // 4, axial_factor)
    angular = across_theta(velocity, angle_slopes)
    axial = lax.all_to_all(
        along_axis(
            lax.all_to_all(velocity, "plane", split_axis=2, concat_axis=1, tiled=True), axis_slopes
        ),
        "plane",
        split_axis=1,
        concat_axis=2,
        tiled=True,
    )
    strain, magnitude = strain_rate(velocity, radial, angular, axial, own_radius)
    scaled = magnitude[None] * strain
    products = jnp.concatenate([velocity, pair_products(velocity), strain, scaled], 0)
    filtered = along_axis(
        lax.all_to_all(
            across_theta(products, angle_smooth), "plane", split_axis=2, concat_axis=1, tiled=True
        ),
        axis_smooth,
    )
    cross_sum, model_sum = shell_terms(filtered)
    cross_sum, model_sum = lax.psum((cross_sum, model_sum), "plane")
    points = NZ * NT
    coefficient = cross_sum / points / (model_sum / points + 1e-06)
    stress = (-2.0 * coefficient * scaled).astype(jnp.bfloat16)
    convection = -step_time * advection(velocity, radial, angular, axial, own_radius)
    return (convection, stress)


def solution(mesh):
    return jax.shard_map(
        shards,
        mesh=mesh,
        in_specs=(P(None, "plane", None, "rad"),),
        out_specs=(P(None, "plane", None, "rad"), P(None, "plane", None, "rad")),
        check_vma=False,
    )
```

profile of v0, /device:TPU:32, one launch (start us, length us, event | category | flops | bytes accessed | tf_op | source)
XLA Modules:
  0.0 770.5 jit_solution(14270530483547991735)
XLA Ops:
  8.1 20.4 %all-gather.2.cloned.1.call-done = f32[3,1,768,256]{3,2,0,1:T(8,128)} async-done(((f32[3,1,768,128]{3,2,0,1:T(8,128)}), f32[3,1,768,256]{3,2,0,1:T(8,128)}) %all-gather.2.cloned.1.call-update) | async-done | bytes 2359312 | tf_op jit(solution)/shard_map/all_gather | solution.py:125
  28.4 5.6 bitcast_dynamic-update-slice_fusion
  34.0 2.6 copy.54
  36.7 13.7 %all-to-all-start = ((f32[3,1,768,128]{3,1,0,2:T(1,128)}), f32[3,1,768,128]{3,1,0,2:T(1,128)S(1)}, u32[]{:S(2)}, u32[]{:S(2)}) async-start(f32[3,1,768,128]{3,1,0,2:T(1,128)} %copy.54), calls=%async_computation | async-start | bytes 2359296 | tf_op jit(solution)/shard_map/all_to_all | solution.py:133
  50.8 19.2 %fusion.219 = f32[768,768,1]{1,0,2:T(8,128)} fusion(), kind=kLoop, calls=%fused_computation.23.clone.clone.1 | loop fusion | flops 13565952 | bytes 2359296 | tf_op jit(solution)/shard_map/jk,fzkr->fzjr/dot_general | solution.py:57
  72.3 12.7 %all-to-all-done = f32[3,1,768,128]{3,1,0,2:T(1,128)S(1)} async-done(((f32[3,1,768,128]{3,1,0,2:T(1,128)}), f32[3,1,768,128]{3,1,0,2:T(1,128)S(1)}, u32[]{:S(2)}, u32[]{:S(2)}) %all-to-all-start) | async-done | bytes 1179680 | tf_op jit(solution)/shard_map/all_to_all | solution.py:133
  85.2 2.3 convolution_bitcast_fusion
  89.1 7.8 %all-to-all-start.1 = ((f32[3,128,6,128]{3,2,0,1:T(8,128)}), f32[3,128,6,128]{3,2,0,1:T(8,128)}, u32[]{:S(2)}, u32[]{:S(2)}) async-start(f32[3,128,6,128]{3,2,0,1:T(8,128)} %copy.57), calls=%async_computation.1 | async-start | bytes 3145728 | tf_op jit(solution)/shard_map/all_to_all | solution.py:131
  99.4 2.9 fusion.60
  103.2 14.7 %fusion.57 = f32[3,1,768,128]{2,3,1,0:T(8,128)S(1)} fusion(f32[128,3,768]{2,0,1:T(8,128)S(1)} %get-tuple-element.30), kind=kOutput, calls=%fused_computation.59 | convolution fusion | flops 2733834240 | bytes 2359296 | tf_op jit(solution)/shard_map/jk,fzkr->fzjr/dot_general | solution.py:57
  119.8 18.6 %all-to-all-done.1 = f32[3,128,6,128]{3,2,0,1:T(8,128)} async-done(((f32[3,128,6,128]{3,2,0,1:T(8,128)}), f32[3,128,6,128]{3,2,0,1:T(8,128)}, u32[]{:S(2)}, u32[]{:S(2)}) %all-to-all-start.1) | async-done | bytes 1179680 | tf_op jit(solution)/shard_map/all_to_all | solution.py:131
  138.4 2.6 fusion.215
  140.9 2.2 slice.123
  143.1 1.9 copy.65
  146.9 2.3 constant_dynamic-update-slice_fusion.4
  149.2 2.2 squeeze.15
  151.4 1.9 copy.58
  153.3 2.2 squeeze.20
  155.5 1.9 copy.62
  158.5 1.9 bitcast_dynamic-update-slice_fusion.1
  166.0 23.8 %fusion.7 = f32[21,1,768,128]{2,3,0,1:T(8,128)} fusion(f32[21,1,768,128]{2,3,1,0:T(8,128)} %multiply_dynamic-update-slice_fusion, f32[768,768,1]{1,0,2:T(8,128)S(1)} %copy-done.5), kind=kOutput, calls=%fused_computation.12 | convolution fusion | flops 19025362944 | bytes 18874368 | tf_op jit(solution)/shard_map/jk,fzkr->fzjr/dot_general | solution.py:57
  189.9 20.4 %copy.66 = f32[21,1,768,128]{3,1,0,2:T(1,128)} copy(f32[21,1,768,128]{2,3,0,1:T(8,128)} %fusion.7) | data formatting | bytes 16515072 | tf_op jit(solution)/shard_map/jk,fzkr->fzjr/transpose | solution.py:57
  210.3 7.8 %all-to-all-start.2 = ((f32[21,1,768,128]{3,1,0,2:T(1,128)}), f32[21,1,768,128]{3,1,0,2:T(1,128)}, u32[]{:S(2)}, u32[]{:S(2)}) async-start(f32[21,1,768,128]{3,1,0,2:T(1,128)} %copy.66), calls=%async_computation.2 | async-start | bytes 16515072 | tf_op jit(solution)/shard_map/all_to_all | solution.py:144
  218.1 2.2 squeeze.17
  220.3 2.2 squeeze.19
  222.5 1.9 copy.59
  224.4 2.1 copy.60
  226.5 2.3 fusion.85
  230.3 170.6 %all-to-all-done.2 = f32[21,1,768,128]{3,1,0,2:T(1,128)} async-done(((f32[21,1,768,128]{3,1,0,2:T(1,128)}), f32[21,1,768,128]{3,1,0,2:T(1,128)}, u32[]{:S(2)}, u32[]{:S(2)}) %all-to-all-start.2) | async-done | bytes 8257568 | tf_op jit(solution)/shard_map/all_to_all | solution.py:144
  400.9 4.0 copy.75
  404.9 10.9 %fusion.4 = f32[21,128,6,128]{3,1,2,0:T(8,128)S(1)} fusion(f32[21,128,6,128]{3,0,2,1:T(8,128)S(1)} %bitcast.130), kind=kOutput, calls=%fused_computation.11 | convolution fusion | flops 3171434496 | bytes 16515072 | tf_op jit(solution)/shard_map/zy,fyab->fzab/dot_general | solution.py:61
  418.2 342.3 %all-reduce = (f32[128]{0:T(128)S(1)}, f32[128]{0:T(128)S(1)}) all-reduce(f32[128]{0:T(128)S(1)} %get-tuple-element.11, f32[128]{0:T(128)S(1)} %get-tuple-element.10), channel_id=1, replica_groups=mesh['plane'=128,'rad'=2] {'plane'}, use_global_device_ids=true, to_apply=%region_5.6 | all-reduce | flops 256 | bytes 2048 | tf_op jit(solution)/shard_map/psum | solution.py:150
  (62 shorter events, 25.8 us)
Async XLA Ops:
  7.2 21.3 %all-gather.2.cloned.1.call-start = ((), (), s32[]{:S(2)}) async-start(), calls=%async_computation.3 | async-start | bytes 3538944 | tf_op jit(solution)/shard_map/all_gather | solution.py:125
  36.7 48.3 %all-to-all-start = ((f32[3,1,768,128]{3,1,0,2:T(1,128)}), f32[3,1,768,128]{3,1,0,2:T(1,128)S(1)}, u32[]{:S(2)}, u32[]{:S(2)}) async-start(f32[3,1,768,128]{3,1,0,2:T(1,128)} %copy.54), calls=%async_computation | async-start | bytes 2359296 | tf_op jit(solution)/shard_map/all_to_all | solution.py:133
  89.1 49.2 %all-to-all-start.1 = ((f32[3,128,6,128]{3,2,0,1:T(8,128)}), f32[3,128,6,128]{3,2,0,1:T(8,128)}, u32[]{:S(2)}, u32[]{:S(2)}) async-start(f32[3,128,6,128]{3,2,0,1:T(8,128)} %copy.57), calls=%async_computation.1 | async-start | bytes 3145728 | tf_op jit(solution)/shard_map/all_to_all | solution.py:131
  97.0 2.4 copy-start.1
  102.3 15.6 %copy-start = (f32[3,768,128]{1,2,0:T(8,128)}, f32[3,768,128]{1,2,0:T(8,128)S(1)}, u32[]{:S(2)}) copy-start(f32[3,768,128]{1,2,0:T(8,128)S(1)} %fusion.60) | copy-start | bytes 3538948
  117.9 1.0 copy-start.2
  145.0 4.1 copy-start.4
  155.5 6.8 copy-start.7
  157.4 3.0 copy-start.6
  162.8 0.8 copy-start.3
  163.5 2.5 copy-start.5
  210.3 190.6 %all-to-all-start.2 = ((f32[21,1,768,128]{3,1,0,2:T(1,128)}), f32[21,1,768,128]{3,1,0,2:T(1,128)}, u32[]{:S(2)}, u32[]{:S(2)}) async-start(f32[21,1,768,128]{3,1,0,2:T(1,128)} %copy.66), calls=%async_computation.2 | async-start | bytes 16515072 | tf_op jit(solution)/shard_map/all_to_all | solution.py:144
  416.2 0.7 copy-start.8
Sparse Core Ops, SparseCore 0:
  9.8 18.6 all-gather.1
where the time goes:
time: 780 us; the launch traced here: 771 us
  blocking collectives  342 us (44%)
  waiting for transfers between devices  223 us (29%)
  local copies, waits for them, and re-layouts  62.1 us (8%)
  matrix products  60.2 us (8%)
  other arithmetic  39 us (5%)
  starting transfers between devices  29.3 us (4%)
  between operations  14.7 us (2%)
    psum x1, blocking collectives, shards(): cross_sum, model_sum = lax.psum((cross_sum, model_sum), 'plane')  342 us
    all_to_all x1, waiting for transfers between devices, shards(): lax.all_to_all(across_theta(products, angle_smooth), 'plane', split_axis=...  171 us
    dot_general x2, matrix products, across_theta(): jnp.einsum('jk,fzkr->fzjr', matrix, fields, precision=lax.Precision.HIGHEST)  38.5 us
    transpose x1, local copies, waits for them, and re-layouts, across_theta(): jnp.einsum('jk,fzkr->fzjr', matrix, fields, precision=lax.Precision.HIGHEST)  20.4 us
    all_gather x1, waiting for transfers between devices, shards(): pieces = lax.all_gather(coefficients, 'rad', axis=3, tiled=True)  20.4 us
    dot_general x1, other arithmetic, across_theta(): jnp.einsum('jk,fzkr->fzjr', matrix, fields, precision=lax.Precision.HIGHEST)  19.2 us
    all_to_all x1, waiting for transfers between devices, shards(): lax.all_to_all(along_axis(lax.all_to_all(velocity, 'plane', split_axis=2,...  18.6 us
  transfers between devices with their start and end apart: 4, of which 4 were waited for; matrix products, arithmetic and copies ran while one was open for 7% of the time, Pallas kernels for 0%

commit v1 on v0

v1 whole, which is shorter than its diff:
```python
import functools

import jax
import jax.numpy as jnp
import ml_dtypes
import numpy as np
from jax import lax
from jax.experimental import pallas as pl
from jax.experimental.pallas import tpu as pltpu
from jax.sharding import PartitionSpec as P

NZ = 128
NT = 768
NR = 256
HALF = 128
FLAT = 3 * NT
KEPT = 64
FIELDS = 21

inner_radius = 1.0
outer_radius = 1.4
axial_factor = 3.0
step_time = 0.002
component_pairs = ((0, 0), (1, 1), (2, 2), (0, 1), (0, 2), (1, 2))
pair_weights = (1.0, 1.0, 1.0, 2.0, 2.0, 2.0)

MESH = pl.DeviceIdType.MESH
f32 = jnp.float32
bf16 = jnp.bfloat16


def two_parts(table):
    table = table.astype(np.float32)
    high = table.astype(ml_dtypes.bfloat16)
    low = (table - high.astype(np.float32)).astype(ml_dtypes.bfloat16)
    return (high, low)


def chebyshev_tables(points):
    degree = np.arange(points, dtype=np.int64)
    angles = np.pi * np.mod(degree[:, None] * degree[None, :], 2 * (points - 1)) / (points - 1)
    node_angles = np.pi * degree / (points - 1)
    inside = (degree > 0) & (degree < points - 1)
    sines = np.where(inside, np.sin(node_angles), 1.0)
    real = degree.astype(np.float64)[:, None]
    parity = np.where(degree % 2 == 0, -1.0, 1.0)[:, None]
    edges = np.where(degree[None, :] == 0, real * real, parity * real * real)
    half_gap = 0.5 * (outer_radius - inner_radius)
    slopes = np.where(inside[None, :], real * np.sin(angles) / sines[None, :], edges) / half_gap
    radius = 0.5 * (inner_radius + outer_radius) + half_gap * np.cos(node_angles)
    return (np.cos(angles), slopes, radius)


def slope_table(points, factor):
    offset = np.arange(points)[:, None] - np.arange(points)[None, :]
    turned = np.pi * offset / points
    diagonal = offset == 0
    sines = np.where(diagonal, 1.0, np.sin(turned))
    parity = np.where(offset % 2 == 0, 0.5, -0.5)
    return np.where(diagonal, 0.0, factor * parity * np.cos(turned) / sines)


def smooth_table(points, keep):
    offset = np.arange(points)[:, None] - np.arange(points)[None, :]
    modes = np.arange(1, keep)
    row = (1.0 + 2.0 * np.cos(2 * np.pi * np.arange(points)[:, None] * modes / points).sum(1)) / points
    return row[np.mod(offset, points)]


def kept_modes(points, keep):
    place = 2 * np.pi * np.arange(points) / points
    table = np.zeros((points, 2 * keep))
    table[:, 0] = np.sqrt(1.0 / points)
    for mode in range(1, keep):
        table[:, 2 * mode - 1] = np.sqrt(2.0 / points) * np.cos(mode * place)
        table[:, 2 * mode] = np.sqrt(2.0 / points) * np.sin(mode * place)
    return table


def all_tables():
    values, slopes, radius = chebyshev_tables(NR)
    blocks = []
    for core in range(2):
        own = slice(core * HALF, (core + 1) * HALF)
        for part in range(2):
            degrees = slice(part * HALF, (part + 1) * HALF)
            blocks += [values[degrees, own].T, slopes[degrees, own].T]
    chebyshev = np.concatenate(blocks, 0)
    modes = kept_modes(NZ, NZ // 4)
    inverse = (1.0 / radius).astype(np.float32)
    return dict(
        cheb=two_parts(chebyshev),
        angle=two_parts(slope_table(NT, 1.0)),
        smooth=two_parts(smooth_table(NT, NT // 4)),
        axis=two_parts(slope_table(NZ, axial_factor)),
        modes=two_parts(modes),
        modes_t=two_parts(np.ascontiguousarray(modes.T)),
        inverse=inverse,
    )


def split(value):
    high = value.astype(bf16)
    return (high, (value - high.astype(f32)).astype(bf16))


def dot3(a, b, by_rows=False):
    dims = (((1,), (1 if by_rows else 0,)), ((), ()))
    one = functools.partial(lax.dot_general, dimension_numbers=dims, preferred_element_type=f32)
    return one(a[0], b[0]) + (one(a[0], b[1]) + one(a[1], b[0]))


def strain_of(velocity, radial, angular, axial, inverse):
    strain = (
        radial[0],
        (angular[1] + velocity[0]) * inverse,
        axial[2],
        0.5 * (radial[1] + (angular[0] - velocity[1]) * inverse),
        0.5 * (axial[0] + radial[2]),
        0.5 * (axial[1] + angular[2] * inverse),
    )
    return (strain, magnitude_of(strain))


def magnitude_of(strain):
    straight = strain[0] * strain[0] + strain[1] * strain[1] + strain[2] * strain[2]
    mixed = strain[3] * strain[3] + strain[4] * strain[4] + strain[5] * strain[5]
    return jnp.sqrt(2.0 * (straight + 2.0 * mixed))


def peer(me, step):
    x = (me // 32 + step // 32) % 4
    y = (me // 8 % 4 + step // 8 % 4) % 4
    z = (me % 8 + step % 8) % 8
    return x * 32 + y * 8 + z


def loop(count, body):
    def step(i, carry):
        body(i)
        return carry

    lax.fori_loop(0, count, step, 0)


def kernel(
    coef, cheb_h, cheb_l, angle_h_hbm, angle_l_hbm, smooth_h_hbm, smooth_l_hbm, axis_h, axis_l, modes_h, modes_l,
    modes_t_h, modes_t_l, inverse_rows, inverse_list,
    conv_out, stress_out,
    own, other, own_h, own_l, other_h, other_l, vel_t, rad_t, vel_z, rad_z, axial_z, axial_r, vel_p, rad_p, ang_p,
    vel_h, vel_l, vz_h, vz_l, ang_z, field_h, field_l, mode_h, mode_l, filtered, scaled, conv, stress, axial_p,
    coefficient_own, coefficient_all, angle_h, angle_l, smooth_h, smooth_l,
    table_sem, in_sem, out_sem, rad_send, rad_recv, vel_send, vel_recv, slope_send, slope_recv, back_send, back_recv,
    coefficient_send, coefficient_recv,
):
    me = lax.axis_index("plane")
    core = lax.axis_index("rad")
    partner = 1 - core

    load = pltpu.make_async_copy(coef, own, in_sem)
    load.start()
    tables = [
        pltpu.make_async_copy(source, place, table_sem.at[i])
        for i, (source, place) in enumerate(
            ((angle_h_hbm, angle_h), (angle_l_hbm, angle_l), (smooth_h_hbm, smooth_h), (smooth_l_hbm, smooth_l))
        )
    ]
    for table in tables:
        table.start()
    barrier = pltpu.get_barrier_semaphore()
    pl.semaphore_signal(barrier, 1, device_id={"rad": partner}, device_id_type=MESH)

    def greet(i):
        pl.semaphore_signal(barrier, 1, device_id={"plane": peer(me, i + 1)}, device_id_type=MESH)

    loop(NZ - 1, greet)
    pl.semaphore_wait(barrier, NZ)
    exchange = pltpu.make_async_remote_copy(
        src_ref=coef, dst_ref=other, send_sem=rad_send, recv_sem=rad_recv, device_id={"rad": partner}, device_id_type=MESH
    )
    exchange.start()

    def cheb(part, first, rows):
        place = pl.ds(pl.multiple_of((core * 2 + part) * 256 + first, HALF), rows)
        return (cheb_h[place, :], cheb_l[place, :])

    def scatter(source, target, send, recv):
        local = pltpu.make_async_copy(source.at[pl.ds(me, 1)], target.at[pl.ds(me, 1)], recv)
        local.start()

        def one(i):
            d = peer(me, i + 1)
            pltpu.make_async_remote_copy(
                src_ref=source.at[pl.ds(d, 1)],
                dst_ref=target.at[pl.ds(me, 1)],
                send_sem=send,
                recv_sem=recv,
                device_id={"plane": d},
                device_id_type=MESH,
            ).start()

        loop(NZ - 1, one)

    def wait_all(target, recv):
        pltpu.make_async_copy(target, target, recv).wait()

    def wait_sent(source, send):
        most = source.at[pl.ds(0, NZ - 8)]
        pltpu.make_async_copy(most, most, send).wait()
        last = source.at[pl.ds(0, 1)]
        for _ in range(7):
            pltpu.make_async_copy(last, last, send).wait()

    load.wait()

    def own_part(i):
        rows = pl.ds(pl.multiple_of(i * 256, 256), 256)
        part = split(own[rows, :])
        own_h[rows, :], own_l[rows, :] = part
        result = dot3(cheb(core, 0, 256), part, True)
        vel_t[:, rows] = result[:HALF]
        rad_t[:, rows] = result[HALF:]

    loop(9, own_part)
    exchange.wait_recv()

    def other_velocity(i):
        rows = pl.ds(pl.multiple_of(i * 256, 256), 256)
        part = split(other[rows, :])
        other_h[rows, :], other_l[rows, :] = part
        vel_t[:, rows] += dot3(cheb(partner, 0, HALF), part, True)

    loop(9, other_velocity)
    scatter(vel_t, vel_z, vel_send, vel_recv)

    def other_slope(i):
        rows = pl.ds(pl.multiple_of(i * 256, 256), 256)
        rad_t[:, rows] += dot3(cheb(partner, HALF, HALF), (other_h[rows, :], other_l[rows, :]), True)

    loop(9, other_slope)
    scatter(rad_t, rad_z, slope_send, slope_recv)

    for c in range(3):
        lanes = slice(c * HALF, (c + 1) * HALF)

        def plane_part(i, c=c, lanes=lanes):
            rows = pl.ds(pl.multiple_of(c * NT + i * 256, 256), 256)
            place = pl.ds(pl.multiple_of(i * 256, 256), 256)
            result = dot3((own_h[rows, :], own_l[rows, :]), cheb(core, 0, 256), True)
            result += dot3((other_h[rows, :], other_l[rows, :]), cheb(partner, 0, 256), True)
            vel_p[place, lanes] = result[:, :HALF]
            rad_p[place, lanes] = result[:, HALF:]
            vel_h[place, lanes], vel_l[place, lanes] = split(result[:, :HALF])

        loop(3, plane_part)

    for table in tables:
        table.wait()

    def plane_angle(i):
        rows = pl.ds(pl.multiple_of(i * 256, 256), 256)
        ang_p[rows, :] = dot3((angle_h[rows, :], angle_l[rows, :]), (vel_h[...], vel_l[...]))

    loop(3, plane_angle)

    wait_all(vel_z, vel_recv)
    for c in range(3):

        def axial_part(i, c=c):
            lanes = pl.ds(pl.multiple_of(c * NT + i * 256, 256), 256)
            part = split(vel_z[:, lanes])
            place = pl.ds(pl.multiple_of(i * 256, 256), 256)
            vz_h[c * NZ : (c + 1) * NZ, place], vz_l[c * NZ : (c + 1) * NZ, place] = part
            axial_z[:, lanes] = dot3((axis_h[...], axis_l[...]), part)

        loop(3, axial_part)
    scatter(axial_z, axial_r, back_send, back_recv)

    def shell_angle(i):
        lanes = pl.ds(pl.multiple_of(i * 256, 256), 256)
        ang_z[:, lanes] = -dot3((vz_h[...], vz_l[...]), (angle_h[:, lanes], angle_l[:, lanes]))

    loop(3, shell_angle)
    wait_all(rad_z, slope_recv)
    inverse = inverse_list[core * HALF + me]

    def shell_products(i):
        rows = pl.ds(pl.multiple_of(i * 16, 16), 16)
        for block in range(3):
            lanes = slice(block * 256, (block + 1) * 256)
            flat = [slice(c * NT + block * 256, c * NT + (block + 1) * 256) for c in range(3)]
            velocity = [vel_z[rows, flat[c]] for c in range(3)]
            radial = [rad_z[rows, flat[c]] for c in range(3)]
            axial = [axial_z[rows, flat[c]] for c in range(3)]
            angular = [ang_z[pl.ds(pl.multiple_of(c * NZ + i * 16, 16), 16), lanes] for c in range(3)]
            strain, magnitude = strain_of(velocity, radial, angular, axial, inverse)
            fields = velocity + [velocity[a] * velocity[b] for a, b in component_pairs]
            fields += list(strain) + [magnitude * s for s in strain]
            for f, field in enumerate(fields):
                place = pl.ds(pl.multiple_of(f * NZ + i * 16, 16), 16)
                field_h[place, lanes], field_l[place, lanes] = split(field)

    loop(NZ // 16, shell_products)

    def to_modes(f):
        rows = pl.ds(pl.multiple_of(f * NZ, NZ), NZ)
        place = pl.ds(pl.multiple_of(f * KEPT, KEPT), KEPT)
        for block in range(3):
            lanes = slice(block * 256, (block + 1) * 256)
            result = dot3((modes_t_h[...], modes_t_l[...]), (field_h[rows, lanes], field_l[rows, lanes]))
            mode_h[place, lanes], mode_l[place, lanes] = split(result)

    loop(FIELDS, to_modes)

    def smooth_group(g):
        rows = pl.ds(pl.multiple_of(g * 448, 64), 448)
        for block in range(3):
            lanes = slice(block * 256, (block + 1) * 256)
            result = dot3((mode_h[rows, :], mode_l[rows, :]), (smooth_h[:, lanes], smooth_l[:, lanes]))
            field_h[rows, lanes], field_l[rows, lanes] = split(result)

    loop(3, smooth_group)

    def from_modes(f):
        rows = pl.ds(pl.multiple_of(f * NZ, NZ), NZ)
        place = pl.ds(pl.multiple_of(f * KEPT, KEPT), KEPT)
        for block in range(3):
            lanes = slice(block * 256, (block + 1) * 256)
            filtered[rows, lanes] = dot3((modes_h[...], modes_l[...]), (field_h[place, lanes], field_l[place, lanes]))

    loop(FIELDS, from_modes)

    def shell_sums(i, sums):
        cross, model_sum = sums
        for block in range(3):
            lanes = slice(block * 256, (block + 1) * 256)
            mean = [filtered[pl.ds(pl.multiple_of(f * NZ + i * 8, 8), 8), lanes] for f in range(FIELDS)]
            magnitude = magnitude_of(mean[9:15])
            for n, (a, b) in enumerate(component_pairs):
                leonard = mean[3 + n] - mean[a] * mean[b]
                model = 2.0 * (mean[15 + n] - 4.0 * (magnitude * mean[9 + n]))
                weighted = model * pair_weights[n]
                cross = cross + leonard * weighted
                model_sum = model_sum + model * weighted
        return (cross, model_sum)

    zero = jnp.zeros((8, 256), f32)
    cross, model_sum = lax.fori_loop(0, NZ // 8, shell_sums, (zero, zero))

    def total(value):
        return jnp.sum(jnp.sum(value, axis=1, keepdims=True), axis=0, keepdims=True)

    points = NZ * NT
    coefficient = (total(cross) / points) / (total(model_sum) / points + 1e-06)
    coefficient_own[...] = jnp.broadcast_to(coefficient, (8, 128))

    def share(i):
        pltpu.make_async_remote_copy(
            src_ref=coefficient_own.at[pl.ds(0, 1)],
            dst_ref=coefficient_all.at[pl.ds(me, 1)],
            send_sem=coefficient_send,
            recv_sem=coefficient_recv,
            device_id={"plane": peer(me, i + 1)},
            device_id_type=MESH,
        ).start()

    pltpu.make_async_copy(
        coefficient_own.at[pl.ds(0, 1)], coefficient_all.at[pl.ds(me, 1)], coefficient_recv
    ).start()
    loop(NZ - 1, share)

    wait_all(axial_r, back_recv)
    for c in range(3):
        for block in range(6):
            first = c * NT + block * 128
            axial_p[block * 128 : (block + 1) * 128, c * HALF : (c + 1) * HALF] = axial_r[:, first : first + 128].T
    inverse_row = inverse_rows[pl.ds(core, 1), :]

    def plane_fields(i):
        rows = pl.ds(pl.multiple_of(i * 16, 16), 16)
        velocity, radial, angular, axial = (
            [ref[rows, c * HALF : (c + 1) * HALF] for c in range(3)] for ref in (vel_p, rad_p, ang_p, axial_p)
        )
        around = jnp.broadcast_to(inverse_row, (16, HALF))
        strain, magnitude = strain_of(velocity, radial, angular, axial, around)
        carried = velocity[1] * around
        parts = [velocity[0] * radial[c] + carried * angular[c] + velocity[2] * axial[c] for c in range(3)]
        parts[0] = parts[0] - velocity[1] * carried
        parts[1] = parts[1] + velocity[0] * carried
        for c in range(3):
            conv[pl.ds(pl.multiple_of(c * NT + i * 16, 16), 16), :] = -step_time * parts[c]
        for n in range(6):
            scaled[pl.ds(pl.multiple_of(n * NT + i * 16, 16), 16), :] = magnitude * strain[n]

    loop(NT // 16, plane_fields)
    conv_copy = pltpu.make_async_copy(conv, conv_out, out_sem.at[0])
    conv_copy.start()
    wait_all(coefficient_all, coefficient_recv)
    factor = -2.0 * coefficient_all[...].T[0:1, :]

    def plane_stress(i):
        rows = pl.ds(pl.multiple_of(i * 64, 64), 64)
        stress[rows, :] = (scaled[rows, :] * jnp.broadcast_to(factor, (64, HALF))).astype(bf16)

    loop(6 * NT // 64, plane_stress)
    stress_copy = pltpu.make_async_copy(stress, stress_out, out_sem.at[1])
    stress_copy.start()

    exchange.wait_send()
    wait_sent(vel_t, vel_send)
    wait_sent(rad_t, slope_send)
    wait_sent(axial_z, back_send)
    wait_sent(coefficient_all, coefficient_send)
    conv_copy.wait()
    stress_copy.wait()


def shards(coefficients):
    tables = all_tables()
    hbm = pl.BlockSpec(memory_space=pl.ANY)
    vmem = pl.BlockSpec(memory_space=pltpu.VMEM)
    smem = pl.BlockSpec(memory_space=pltpu.SMEM)
    flat = [FLAT, HALF]
    shell = [NZ, FLAT]
    plane = [NT, 3 * HALF]
    semaphore = pltpu.SemaphoreType.DMA
    scratch = [
        (flat, f32), (flat, f32), (flat, bf16), (flat, bf16), (flat, bf16), (flat, bf16),
        (shell, f32), (shell, f32), (shell, f32), (shell, f32), (shell, f32), (shell, f32),
        (plane, f32), (plane, f32), (plane, f32), (plane, bf16), (plane, bf16),
        ([3 * NZ, NT], bf16), ([3 * NZ, NT], bf16), ([3 * NZ, NT], f32),
        ([FIELDS * NZ, NT], bf16), ([FIELDS * NZ, NT], bf16),
        ([FIELDS * KEPT, NT], bf16), ([FIELDS * KEPT, NT], bf16),
        ([FIELDS * NZ, NT], f32), ([6 * NT, HALF], f32), (flat, f32), ([6 * NT, HALF], bf16), (plane, f32),
        ([8, 128], f32), ([NZ, 128], f32),
        ([NT, NT], bf16), ([NT, NT], bf16), ([NT, NT], bf16), ([NT, NT], bf16),
    ]
    inverse = tables["inverse"]
    rows = np.zeros((8, HALF), np.float32)
    rows[:2] = inverse.reshape(2, HALF)
    operands = [coefficients.reshape(FLAT, HALF)]
    specs = [hbm]
    for name, spec in (("cheb", vmem), ("angle", hbm), ("smooth", hbm), ("axis", vmem), ("modes", vmem), ("modes_t", vmem)):
        operands += [jnp.asarray(part) for part in tables[name]]
        specs += [spec, spec]
    operands += [jnp.asarray(rows), jnp.asarray(inverse)]
    specs += [vmem, smem]
    convection, stress = pl.pallas_call(
        kernel,
        out_shape=(jax.ShapeDtypeStruct((FLAT, HALF), f32), jax.ShapeDtypeStruct((6 * NT, HALF), bf16)),
        in_specs=specs,
        out_specs=(hbm, hbm),
        scratch_shapes=[pltpu.VMEM(tuple(shape), kind) for shape, kind in scratch]
        + [semaphore((4,)), semaphore, semaphore((2,))]
        + [semaphore] * 10,
        compiler_params=pltpu.CompilerParams(collective_id=0, has_side_effects=True, vmem_limit_bytes=60 << 20),
    )(*operands)
    return (convection.reshape(3, 1, NT, HALF), stress.reshape(6, 1, NT, HALF))


def solution(mesh):
    return jax.shard_map(
        shards,
        mesh=mesh,
        in_specs=(P(None, "plane", None, "rad"),),
        out_specs=(P(None, "plane", None, "rad"), P(None, "plane", None, "rad")),
        check_vma=False,
    )
```

time: 780 us -> 114 us (0.15); the launches traced: 771 us -> 112 us
  blocking collectives: 342 us -> 0 us
  waiting for transfers between devices: 223 us -> 0 us
  Pallas kernels: 0 us -> 108 us
  matrix products: 60.2 us -> 0 us
  local copies, waits for them, and re-layouts: 62.1 us -> 3.47 us
  other arithmetic: 39 us -> 0 us
  starting transfers between devices: 29.3 us -> 0 us
  between operations: 14.7 us -> 0.65 us
    psum x1 -> x0, blocking collectives: 342 us -> none  [shards(): cross_sum, model_sum = lax.psum((cross_sum, model_sum), 'plane')]
    all_to_all x3 -> x0, waiting for transfers between devices: 202 us -> none  [the longest x1 171 us: shards(): lax.all_to_all(across_theta(products, angle_smooth), 'plane', split_axis=...]
    pallas_call x0 -> x1, Pallas kernels: none -> 108 us  [shards(): pl.pallas_call(kernel, out_shape=(jax.ShapeDtypeStruct((FLAT, HALF), f32)...]
    dot_general x6 -> x0, matrix products: 60.2 us -> none  [the longest x2 38.5 us: across_theta(): jnp.einsum('jk,fzkr->fzjr', matrix, fields, precision=lax.Precision.HIGHEST)]
    all_to_all x3 -> x0, starting transfers between devices: 29.3 us -> none  [the longest x1 13.7 us: shards(): lax.all_to_all(velocity, 'plane', split_axis=2, concat_axis=1, tiled=True)]
    transpose x2 -> x0, local copies, waits for them, and re-layouts: 22.1 us -> none  [the longest x1 20.4 us: across_theta(): jnp.einsum('jk,fzkr->fzjr', matrix, fields, precision=lax.Precision.HIGHEST)]
    all_gather x1 -> x0, waiting for transfers between devices: 20.4 us -> none  [shards(): pieces = lax.all_gather(coefficients, 'rad', axis=3, tiled=True)]
    dot_general x1 -> x0, other arithmetic: 19.2 us -> none  [across_theta(): jnp.einsum('jk,fzkr->fzjr', matrix, fields, precision=lax.Precision.HIGHEST)]
  transfers between devices with their start and end apart: 4 -> 0, of which waited for: 4 -> 0; matrix products, arithmetic and copies ran while one was open for 7% -> 0% of each run, Pallas kernels for 0% -> 0%
where the time goes in v1:
time: 114 us; the launch traced here: 112 us
  Pallas kernels  108 us (95%)
  local copies, waits for them, and re-layouts  3.47 us (3%)
    pallas_call x1, Pallas kernels, shards(): pl.pallas_call(kernel, out_shape=(jax.ShapeDtypeStruct((FLAT, HALF), f32)...  108 us
    unnamed x4, local copies, waits for them, and re-layouts  3.47 us

profile of v1, /device:TPU:32, one launch (start us, length us, event | category | flops | bytes accessed | tf_op | source)
XLA Modules:
  0.0 112.5 jit_solution(15588903620668904992)
XLA Ops:
  0.6 108.3 %shard_map.158 = (f32[2304,128]{1,0:T(8,128)}, bf16[4608,128]{1,0:T(8,128)(2,1)}) custom-call(f32[2304,128]{1,0:T(8,128)} %bitcast.9, bf16[1024,128]{1,0:T(8,128)(2,1)} %constant.28.clone.cheb_h, bf16[1024,128]{1,0:T(8,128)(2,1)} %constant.29.clone.cheb_l, bf16[768,768]{1,0:T(8,128)(2,1)} %constant.30.clone.angle_h_hbm, ...), custom_call_target="tpu_custom_call" | custom-call | tf_op jit(solution)/shard_map/pallas_call | solution.py:448
  109.0 0.0 copy-start
  109.0 2.5 %copy.21 = f32[3,1,768,128]{3,2,1,0:T(8,128)} copy(f32[3,1,768,128]{3,2,1,0:T(8,128)} %bitcast.8) | data formatting | bytes 2359296
  111.4 0.0 copy-done
  111.5 1.0 copy.22
Async XLA Ops:
  109.0 2.5 %copy-start = (bf16[4608,128]{1,0:T(8,128)(2,1)S(1)}, bf16[4608,128]{1,0:T(8,128)(2,1)}, u32[]{:S(2)}) copy-start(bf16[4608,128]{1,0:T(8,128)(2,1)} %get-tuple-element.5) | copy-start | bytes 3538948

commit v2 on v1

--- a/solution.py
+++ b/solution.py
@@ -128,11 +128,27 @@
     return jnp.sqrt(2.0 * (straight + 2.0 * mixed))
 
 
-def peer(me, step):
-    x = (me // 32 + step // 32) % 4
-    y = (me // 8 % 4 + step // 8 % 4) % 4
-    z = (me % 8 + step % 8) % 8
-    return x * 32 + y * 8 + z
+def flipped(value, mask, size):
+    total, bit = 0, 1
+    while bit < size:
+        a, b = value // bit % 2, mask // bit % 2
+        total = total + (a + b - 2 * a * b) * bit
+        bit *= 2
+    return total
+
+
+def each_peer(me, body):
+    low = [flipped(me % 8, k, 8) for k in range(8)]
+    own = me // 8
+    for k in range(1, 8):
+        body(own * 8 + low[k])
+
+    def group(i):
+        first = flipped(own, i + 1, 16) * 8
+        for k in range(8):
+            body(first + low[k])
+
+    loop(NZ // 8 - 1, group)
 
 
 def loop(count, body):
@@ -146,12 +162,12 @@
 def kernel(
     coef, cheb_h, cheb_l, angle_h_hbm, angle_l_hbm, smooth_h_hbm, smooth_l_hbm, axis_h, axis_l, modes_h, modes_l,
     modes_t_h, modes_t_l, inverse_rows, inverse_list,
-    conv_out, stress_out,
+    conv_out, scaled_out, factor_out,
     own, other, own_h, own_l, other_h, other_l, vel_t, rad_t, vel_z, rad_z, axial_z, axial_r, vel_p, rad_p, ang_p,
-    vel_h, vel_l, vz_h, vz_l, ang_z, field_h, field_l, mode_h, mode_l, filtered, scaled, conv, stress, axial_p,
+    vel_h, vel_l, vz_h, vz_l, ang_z, field_h, field_l, mode_h, mode_l, filtered, scaled, conv, axial_p,
     coefficient_own, coefficient_all, angle_h, angle_l, smooth_h, smooth_l,
     table_sem, in_sem, out_sem, rad_send, rad_recv, vel_send, vel_recv, slope_send, slope_recv, back_send, back_recv,
-    coefficient_send, coefficient_recv,
+    coefficient_send, coefficient_recv, in_y, in_x,
 ):
     me = lax.axis_index("plane")
     core = lax.axis_index("rad")
@@ -167,39 +183,53 @@
     ]
     for table in tables:
         table.start()
+    x, y, z = me // 32, me // 8 % 4, me % 8
+    along_z = [x * 32 + y * 8 + (z + k) % 8 for k in range(1, 8)]
+    along_y = [x * 32 + (y + k) % 4 * 8 + z for k in range(1, 4)]
+    along_x = [(x + k) % 4 * 32 + y * 8 + z for k in range(1, 4)]
+
+    def greet(semaphore, places):
+        for place in places:
+            pl.semaphore_signal(semaphore, 1, device_id={"plane": place}, device_id_type=MESH)
+
     barrier = pltpu.get_barrier_semaphore()
     pl.semaphore_signal(barrier, 1, device_id={"rad": partner}, device_id_type=MESH)
-
-    def greet(i):
-        pl.semaphore_signal(barrier, 1, device_id={"plane": peer(me, i + 1)}, device_id_type=MESH)
-
-    loop(NZ - 1, greet)
-    pl.semaphore_wait(barrier, NZ)
-    exchange = pltpu.make_async_remote_copy(
-        src_ref=coef, dst_ref=other, send_sem=rad_send, recv_sem=rad_recv, device_id={"rad": partner}, device_id_type=MESH
-    )
-    exchange.start()
+    greet(barrier, along_z + along_y + along_x)
+    pl.semaphore_wait(barrier, 14)
+    exchanges = [
+        pltpu.make_async_remote_copy(
+            src_ref=coef.at[pl.ds(c * NT, NT)],
+            dst_ref=other.at[pl.ds(c * NT, NT)],
+            send_sem=rad_send.at[c],
+            recv_sem=rad_recv.at[c],
+            device_id={"rad": partner},
+            device_id_type=MESH,
+        )
+        for c in range(3)
+    ]
+    for exchange in exchanges:
+        exchange.start()
+    greet(in_y, along_y)
 
     def cheb(part, first, rows):
         place = pl.ds(pl.multiple_of((core * 2 + part) * 256 + first, HALF), rows)
         return (cheb_h[place, :], cheb_l[place, :])
 
-    def scatter(source, target, send, recv):
-        local = pltpu.make_async_copy(source.at[pl.ds(me, 1)], target.at[pl.ds(me, 1)], recv)
+    def scatter(source, target, send, recv, lanes=slice(None)):
+        local = pltpu.make_async_copy(source.at[pl.ds(me, 1), lanes], target.at[pl.ds(me, 1), lanes], recv)
         local.start()
 
-        def one(i):
-            d = peer(me, i + 1)
+        def one(d):
             pltpu.make_async_remote_copy(
-                src_ref=source.at[pl.ds(d, 1)],
-                dst_ref=target.at[pl.ds(me, 1)],
+                src_ref=source.at[pl.ds(d, 1), lanes],
+                dst_ref=target.at[pl.ds(me, 1), lanes],
                 send_sem=send,
                 recv_sem=recv,
                 device_id={"plane": d},
                 device_id_type=MESH,
             ).start()
 
-        loop(NZ - 1, one)
+        each_peer(me, one)
 
     def wait_all(target, recv):
         pltpu.make_async_copy(target, target, recv).wait()
@@ -221,8 +251,10 @@
         vel_t[:, rows] = result[:HALF]
         rad_t[:, rows] = result[HALF:]
 
-    loop(9, own_part)
-    exchange.wait_recv()
+    loop(3, own_part)
+    pl.semaphore_wait(in_y, 3)
+    greet(in_x, along_x)
+    loop(6, lambda i: own_part(i + 3))
 
     def other_velocity(i):
         rows = pl.ds(pl.multiple_of(i * 256, 256), 256)
@@ -230,7 +262,10 @@
         other_h[rows, :], other_l[rows, :] = part
         vel_t[:, rows] += dot3(cheb(partner, 0, HALF), part, True)
 
-    loop(9, other_velocity)
+    for c in range(3):
+        exchanges[c].wait_recv()
+        loop(3, lambda i, c=c: other_velocity(i + 3 * c))
+    pl.semaphore_wait(in_x, 3)
     scatter(vel_t, vel_z, vel_send, vel_recv)
 
     def other_slope(i):
@@ -264,17 +299,18 @@
     loop(3, plane_angle)
 
     wait_all(vel_z, vel_recv)
-    for c in range(3):
-
-        def axial_part(i, c=c):
-            lanes = pl.ds(pl.multiple_of(c * NT + i * 256, 256), 256)
+    for block in range(3):
+
+        def axial_part(c, block=block):
+            lanes = pl.ds(pl.multiple_of(c * NT + block * 256, 256), 256)
             part = split(vel_z[:, lanes])
-            place = pl.ds(pl.multiple_of(i * 256, 256), 256)
-            vz_h[c * NZ : (c + 1) * NZ, place], vz_l[c * NZ : (c + 1) * NZ, place] = part
-            axial_z[:, lanes] = dot3((axis_h[...], axis_l[...]), part)
+            rows = pl.ds(pl.multiple_of(c * NZ, NZ), NZ)
+            vz_h[rows, block * 256 : (block + 1) * 256], vz_l[rows, block * 256 : (block + 1) * 256] = part
+            place = pl.ds(pl.multiple_of(block * NT + c * 256, 256), 256)
+            axial_z[:, place] = dot3((axis_h[...], axis_l[...]), part)
 
         loop(3, axial_part)
-    scatter(axial_z, axial_r, back_send, back_recv)
+        scatter(axial_z, axial_r, back_send.at[block], back_recv.at[block], pl.ds(block * NT, NT))
 
     def shell_angle(i):
         lanes = pl.ds(pl.multiple_of(i * 256, 256), 256)
@@ -291,7 +327,7 @@
             flat = [slice(c * NT + block * 256, c * NT + (block + 1) * 256) for c in range(3)]
             velocity = [vel_z[rows, flat[c]] for c in range(3)]
             radial = [rad_z[rows, flat[c]] for c in range(3)]
-            axial = [axial_z[rows, flat[c]] for c in range(3)]
+            axial = [axial_z[rows, block * NT + c * 256 : block * NT + (c + 1) * 256] for c in range(3)]
             angular = [ang_z[pl.ds(pl.multiple_of(c * NZ + i * 16, 16), 16), lanes] for c in range(3)]
             strain, magnitude = strain_of(velocity, radial, angular, axial, inverse)
             fields = velocity + [velocity[a] * velocity[b] for a, b in component_pairs]
@@ -354,65 +390,71 @@
     coefficient = (total(cross) / points) / (total(model_sum) / points + 1e-06)
     coefficient_own[...] = jnp.broadcast_to(coefficient, (8, 128))
 
-    def share(i):
+    def share(d):
         pltpu.make_async_remote_copy(
             src_ref=coefficient_own.at[pl.ds(0, 1)],
             dst_ref=coefficient_all.at[pl.ds(me, 1)],
             send_sem=coefficient_send,
             recv_sem=coefficient_recv,
-            device_id={"plane": peer(me, i + 1)},
+            device_id={"plane": d},
             device_id_type=MESH,
         ).start()
 
     pltpu.make_async_copy(
         coefficient_own.at[pl.ds(0, 1)], coefficient_all.at[pl.ds(me, 1)], coefficient_recv
     ).start()
-    loop(NZ - 1, share)
-
-    wait_all(axial_r, back_recv)
-    for c in range(3):
-        for block in range(6):
-            first = c * NT + block * 128
-            axial_p[block * 128 : (block + 1) * 128, c * HALF : (c + 1) * HALF] = axial_r[:, first : first + 128].T
+    each_peer(me, share)
+
     inverse_row = inverse_rows[pl.ds(core, 1), :]
 
     def plane_fields(i):
-        rows = pl.ds(pl.multiple_of(i * 16, 16), 16)
+        rows = pl.ds(pl.multiple_of(i * 32, 32), 32)
         velocity, radial, angular, axial = (
             [ref[rows, c * HALF : (c + 1) * HALF] for c in range(3)] for ref in (vel_p, rad_p, ang_p, axial_p)
         )
-        around = jnp.broadcast_to(inverse_row, (16, HALF))
+        around = jnp.broadcast_to(inverse_row, (32, HALF))
         strain, magnitude = strain_of(velocity, radial, angular, axial, around)
         carried = velocity[1] * around
         parts = [velocity[0] * radial[c] + carried * angular[c] + velocity[2] * axial[c] for c in range(3)]
         parts[0] = parts[0] - velocity[1] * carried
         parts[1] = parts[1] + velocity[0] * carried
         for c in range(3):
-            conv[pl.ds(pl.multiple_of(c * NT + i * 16, 16), 16), :] = -step_time * parts[c]
+            conv[pl.ds(pl.multiple_of(c * NT + i * 32, 32), 32), :] = -step_time * parts[c]
         for n in range(6):
-            scaled[pl.ds(pl.multiple_of(n * NT + i * 16, 16), 16), :] = magnitude * strain[n]
-
-    loop(NT // 16, plane_fields)
-    conv_copy = pltpu.make_async_copy(conv, conv_out, out_sem.at[0])
-    conv_copy.start()
+            scaled[pl.ds(pl.multiple_of(n * NT + i * 32, 32), 32), :] = magnitude * strain[n]
+
+    for block in range(3):
+        arrived = axial_r.at[:, pl.ds(block * NT, NT)]
+        wait_all(arrived, back_recv.at[block])
+        for c in range(3):
+            for half in range(2):
+                first = block * NT + c * 256 + half * 128
+                rows = slice(block * 256 + half * 128, block * 256 + (half + 1) * 128)
+                axial_p[rows, c * HALF : (c + 1) * HALF] = axial_r[:, first : first + 128].T
+        loop(8, lambda i, block=block: plane_fields(i + 8 * block))
+        for n in range(3):
+            rows = pl.ds(n * NT + block * 256, 256)
+            pltpu.make_async_copy(conv.at[rows], conv_out.at[rows], out_sem.at[0]).start()
+        for n in range(6):
+            rows = pl.ds(n * NT + block * 256, 256)
+            pltpu.make_async_copy(scaled.at[rows], scaled_out.at[rows], out_sem.at[1]).start()
     wait_all(coefficient_all, coefficient_recv)
-    factor = -2.0 * coefficient_all[...].T[0:1, :]
-
-    def plane_stress(i):
-        rows = pl.ds(pl.multiple_of(i * 64, 64), 64)
-        stress[rows, :] = (scaled[rows, :] * jnp.broadcast_to(factor, (64, HALF))).astype(bf16)
-
-    loop(6 * NT // 64, plane_stress)
-    stress_copy = pltpu.make_async_copy(stress, stress_out, out_sem.at[1])
-    stress_copy.start()
-
-    exchange.wait_send()
+    factor_out[...] = jnp.broadcast_to(-2.0 * coefficient_all[...].T[0:1, :], (8, HALF))
+
+    for exchange in exchanges:
+        exchange.wait_send()
     wait_sent(vel_t, vel_send)
     wait_sent(rad_t, slope_send)
-    wait_sent(axial_z, back_send)
+    for block in range(3):
+        wait_sent(axial_z.at[:, pl.ds(block * NT, NT)], back_send.at[block])
     wait_sent(coefficient_all, coefficient_send)
-    conv_copy.wait()
-    stress_copy.wait()
+    pltpu.make_async_copy(conv, conv_out, out_sem.at[0]).wait()
+    pltpu.make_async_copy(scaled, scaled_out, out_sem.at[1]).wait()
+
+
+def finish(conv_ref, scaled_ref, factor_ref, conv_out, stress_out):
+    conv_out[...] = conv_ref[...]
+    stress_out[...] = (scaled_ref[...] * factor_ref[0:1, :]).astype(bf16)
 
 
 def shards(coefficients):
@@ -431,7 +473,7 @@
         ([3 * NZ, NT], bf16), ([3 * NZ, NT], bf16), ([3 * NZ, NT], f32),
         ([FIELDS * NZ, NT], bf16), ([FIELDS * NZ, NT], bf16),
         ([FIELDS * KEPT, NT], bf16), ([FIELDS * KEPT, NT], bf16),
-        ([FIELDS * NZ, NT], f32), ([6 * NT, HALF], f32), (flat, f32), ([6 * NT, HALF], bf16), (plane, f32),
+        ([FIELDS * NZ, NT], f32), ([6 * NT, HALF], f32), (flat, f32), (plane, f32),
         ([8, 128], f32), ([NZ, 128], f32),
         ([NT, NT], bf16), ([NT, NT], bf16), ([NT, NT], bf16), ([NT, NT], bf16),
     ]
@@ -445,16 +487,34 @@
         specs += [spec, spec]
     operands += [jnp.asarray(rows), jnp.asarray(inverse)]
     specs += [vmem, smem]
-    convection, stress = pl.pallas_call(
+    conv, scaled, factor = pl.pallas_call(
         kernel,
-        out_shape=(jax.ShapeDtypeStruct((FLAT, HALF), f32), jax.ShapeDtypeStruct((6 * NT, HALF), bf16)),
+        out_shape=(jax.ShapeDtypeStruct((FLAT, HALF), f32), jax.ShapeDtypeStruct((6 * NT, HALF), f32),
+                   jax.ShapeDtypeStruct((8, HALF), f32)),
         in_specs=specs,
-        out_specs=(hbm, hbm),
+        out_specs=(hbm, hbm, vmem),
         scratch_shapes=[pltpu.VMEM(tuple(shape), kind) for shape, kind in scratch]
-        + [semaphore((4,)), semaphore, semaphore((2,))]
-        + [semaphore] * 10,
+        + [semaphore((4,)), semaphore, semaphore((2,)), semaphore((3,)), semaphore((3,))]
+        + [semaphore] * 4
+        + [semaphore((3,)), semaphore((3,)), semaphore, semaphore]
+        + [pltpu.SemaphoreType.REGULAR] * 2,
         compiler_params=pltpu.CompilerParams(collective_id=0, has_side_effects=True, vmem_limit_bytes=60 << 20),
     )(*operands)
+    steps = 4
+    convection, stress = pl.pallas_call(
+        finish,
+        grid=(steps,),
+        out_shape=(jax.ShapeDtypeStruct((FLAT, HALF), f32), jax.ShapeDtypeStruct((6 * NT, HALF), bf16)),
+        in_specs=[
+            pl.BlockSpec((FLAT // steps, HALF), lambda i: (i, 0)),
+            pl.BlockSpec((6 * NT // steps, HALF), lambda i: (i, 0)),
+            pl.BlockSpec((8, HALF), lambda i: (0, 0)),
+        ],
+        out_specs=(
+            pl.BlockSpec((FLAT // steps, HALF), lambda i: (i, 0)),
+            pl.BlockSpec((6 * NT // steps, HALF), lambda i: (i, 0)),
+        ),
+    )(conv, scaled, factor)
     return (convection.reshape(3, 1, NT, HALF), stress.reshape(6, 1, NT, HALF))
 
 

time: 114 us -> 106 us (0.930)
  local copies, waits for them, and re-layouts: 3.47 us -> 0 us
  Pallas kernels: 108 us -> 105 us
    pallas_call x1, Pallas kernels: 108 us -> 101 us  [shards(): pl.pallas_call(kernel, out_shape=(jax.ShapeDtypeStruct((FLAT, HALF), f32)...]
    pallas_call x0 -> x1, Pallas kernels: none -> 4.11 us  [shards(): pl.pallas_call(finish, grid=(steps,), out_shape=(jax.ShapeDtypeStruct((FL...]
    unnamed x4 -> x0, local copies, waits for them, and re-layouts: 3.47 us -> none
where the time goes in v2:
time: 106 us; the launch traced here: 105 us
  Pallas kernels  105 us (99%)
    pallas_call x1, Pallas kernels, shards(): pl.pallas_call(kernel, out_shape=(jax.ShapeDtypeStruct((FLAT, HALF), f32)...  101 us
    pallas_call x1, Pallas kernels, shards(): pl.pallas_call(finish, grid=(steps,), out_shape=(jax.ShapeDtypeStruct((FL...  4.11 us

profile of v2, /device:TPU:32, one launch (start us, length us, event | category | flops | bytes accessed | tf_op | source)
XLA Modules:
  0.0 105.3 jit_solution(15772380931952552408)
XLA Ops:
  0.6 100.6 %shard_map.158 = (f32[2304,128]{1,0:T(8,128)}, f32[4608,128]{1,0:T(8,128)}, f32[8,128]{1,0:T(8,128)}) custom-call(f32[2304,128]{1,0:T(8,128)} %bitcast.7, bf16[1024,128]{1,0:T(8,128)(2,1)} %constant.28.clone.cheb_h, bf16[1024,128]{1,0:T(8,128)(2,1)} %constant.29.clone.cheb_l, bf16[768,768]{1,0:T(8,128)(2,1)} %constant.30.clone.angle_h_hbm, ...), custom_call_target="tpu_custom_call" | custom-call | tf_op jit(solution)/shard_map/pallas_call | solution.py:490
  101.2 4.1 %shard_map.159 = (f32[2304,128]{1,0:T(8,128)}, bf16[4608,128]{1,0:T(8,128)(2,1)}) custom-call(f32[2304,128]{1,0:T(8,128)} %get-tuple-element.7.conv_ref, f32[4608,128]{1,0:T(8,128)} %get-tuple-element.8.scaled_ref, f32[8,128]{1,0:T(8,128)} %get-tuple-element.9.factor_ref), custom_call_target="tpu_custom_call" | custom-call | tf_op jit(solution)/shard_map/pallas_call | solution.py:504

commit v3 on v2

--- a/solution.py
+++ b/solution.py
@@ -15,7 +15,12 @@
 HALF = 128
 FLAT = 3 * NT
 KEPT = 64
+PIECES = 6
 FIELDS = 21
+EARLY = 12
+early_strain = (1, 2, 5)
+late_strain = (0, 3, 4)
+strain_places = (12, 9, 10, 13, 14, 11)
 
 inner_radius = 1.0
 outer_radius = 1.4
@@ -111,15 +116,21 @@
 
 
 def strain_of(velocity, radial, angular, axial, inverse):
-    strain = (
-        radial[0],
+    late = (None, None, None)
+    if radial is not None:
+        late = (
+            radial[0],
+            0.5 * (radial[1] + (angular[0] - velocity[1]) * inverse),
+            0.5 * (axial[0] + radial[2]),
+        )
+    return (
+        late[0],
         (angular[1] + velocity[0]) * inverse,
         axial[2],
-        0.5 * (radial[1] + (angular[0] - velocity[1]) * inverse),
-        0.5 * (axial[0] + radial[2]),
+        late[1],
+        late[2],
         0.5 * (axial[1] + angular[2] * inverse),
     )
-    return (strain, magnitude_of(strain))
 
 
 def magnitude_of(strain):
@@ -137,14 +148,14 @@
     return total
 
 
-def each_peer(me, body):
-    low = [flipped(me % 8, k, 8) for k in range(8)]
+def each_peer(me, core, body):
     own = me // 8
     for k in range(1, 8):
-        body(own * 8 + low[k])
+        body(own * 8 + flipped(me % 8, k + core * (8 - 2 * k), 8))
+    low = [flipped(me % 8, k + core * (7 - 2 * k), 8) for k in range(8)]
 
     def group(i):
-        first = flipped(own, i + 1, 16) * 8
+        first = flipped(own, i + 1 + core * (14 - 2 * i), 16) * 8
         for k in range(8):
             body(first + low[k])
 
@@ -164,7 +175,7 @@
     modes_t_h, modes_t_l, inverse_rows, inverse_list,
     conv_out, scaled_out, factor_out,
     own, other, own_h, own_l, other_h, other_l, vel_t, rad_t, vel_z, rad_z, axial_z, axial_r, vel_p, rad_p, ang_p,
-    vel_h, vel_l, vz_h, vz_l, ang_z, field_h, field_l, mode_h, mode_l, filtered, scaled, conv, axial_p,
+    vel_h, vel_l, vz_h, vz_l, ang_z, field_h, field_l, mode_h, mode_l, smoothed_h, smoothed_l, filtered, scaled, conv, axial_p,
     coefficient_own, coefficient_all, angle_h, angle_l, smooth_h, smooth_l,
     table_sem, in_sem, out_sem, rad_send, rad_recv, vel_send, vel_recv, slope_send, slope_recv, back_send, back_recv,
     coefficient_send, coefficient_recv, in_y, in_x,
@@ -229,7 +240,7 @@
                 device_id_type=MESH,
             ).start()
 
-        each_peer(me, one)
+        each_peer(me, core, one)
 
     def wait_all(target, recv):
         pltpu.make_async_copy(target, target, recv).wait()
@@ -265,8 +276,9 @@
     for c in range(3):
         exchanges[c].wait_recv()
         loop(3, lambda i, c=c: other_velocity(i + 3 * c))
-    pl.semaphore_wait(in_x, 3)
-    scatter(vel_t, vel_z, vel_send, vel_recv)
+        if c == 0:
+            pl.semaphore_wait(in_x, 3)
+        scatter(vel_t, vel_z, vel_send.at[c], vel_recv.at[c], pl.ds(c * NT, NT))
 
     def other_slope(i):
         rows = pl.ds(pl.multiple_of(i * 256, 256), 256)
@@ -298,18 +310,19 @@
 
     loop(3, plane_angle)
 
-    wait_all(vel_z, vel_recv)
-    for block in range(3):
-
-        def axial_part(c, block=block):
+    for c in range(3):
+        wait_all(vel_z.at[:, pl.ds(c * NT, NT)], vel_recv.at[c])
+
+        def axial_part(block, c=c):
             lanes = pl.ds(pl.multiple_of(c * NT + block * 256, 256), 256)
             part = split(vel_z[:, lanes])
-            rows = pl.ds(pl.multiple_of(c * NZ, NZ), NZ)
-            vz_h[rows, block * 256 : (block + 1) * 256], vz_l[rows, block * 256 : (block + 1) * 256] = part
+            place = pl.ds(pl.multiple_of(block * 256, 256), 256)
+            vz_h[c * NZ : (c + 1) * NZ, place], vz_l[c * NZ : (c + 1) * NZ, place] = part
             place = pl.ds(pl.multiple_of(block * NT + c * 256, 256), 256)
             axial_z[:, place] = dot3((axis_h[...], axis_l[...]), part)
 
         loop(3, axial_part)
+    for block in range(3):
         scatter(axial_z, axial_r, back_send.at[block], back_recv.at[block], pl.ds(block * NT, NT))
 
     def shell_angle(i):
@@ -317,26 +330,36 @@
         ang_z[:, lanes] = -dot3((vz_h[...], vz_l[...]), (angle_h[:, lanes], angle_l[:, lanes]))
 
     loop(3, shell_angle)
-    wait_all(rad_z, slope_recv)
     inverse = inverse_list[core * HALF + me]
 
-    def shell_products(i):
+    def shell_block(i, block):
         rows = pl.ds(pl.multiple_of(i * 16, 16), 16)
+        lanes = slice(block * 256, (block + 1) * 256)
+        flat = [slice(c * NT + block * 256, c * NT + (block + 1) * 256) for c in range(3)]
+        velocity = [vel_z[rows, flat[c]] for c in range(3)]
+        axial = [axial_z[rows, block * NT + c * 256 : block * NT + (c + 1) * 256] for c in range(3)]
+        angular = [ang_z[pl.ds(pl.multiple_of(c * NZ + i * 16, 16), 16), lanes] for c in range(3)]
+        return rows, lanes, flat, velocity, axial, angular
+
+    def keep(i, lanes, first, fields):
+        for f, field in enumerate(fields):
+            place = pl.ds(pl.multiple_of((first + f) * NZ + i * 16, 16), 16)
+            field_h[place, lanes], field_l[place, lanes] = split(field)
+
+    def early_products(i):
         for block in range(3):
-            lanes = slice(block * 256, (block + 1) * 256)
-            flat = [slice(c * NT + block * 256, c * NT + (block + 1) * 256) for c in range(3)]
-            velocity = [vel_z[rows, flat[c]] for c in range(3)]
+            rows, lanes, flat, velocity, axial, angular = shell_block(i, block)
+            strain = strain_of(velocity, None, angular, axial, inverse)
+            pairs = [velocity[a] * velocity[b] for a, b in component_pairs]
+            keep(i, lanes, 0, velocity + pairs + [strain[n] for n in early_strain])
+
+    def late_products(i):
+        for block in range(3):
+            rows, lanes, flat, velocity, axial, angular = shell_block(i, block)
             radial = [rad_z[rows, flat[c]] for c in range(3)]
-            axial = [axial_z[rows, block * NT + c * 256 : block * NT + (c + 1) * 256] for c in range(3)]
-            angular = [ang_z[pl.ds(pl.multiple_of(c * NZ + i * 16, 16), 16), lanes] for c in range(3)]
-            strain, magnitude = strain_of(velocity, radial, angular, axial, inverse)
-            fields = velocity + [velocity[a] * velocity[b] for a, b in component_pairs]
-            fields += list(strain) + [magnitude * s for s in strain]
-            for f, field in enumerate(fields):
-                place = pl.ds(pl.multiple_of(f * NZ + i * 16, 16), 16)
-                field_h[place, lanes], field_l[place, lanes] = split(field)
-
-    loop(NZ // 16, shell_products)
+            strain = strain_of(velocity, radial, angular, axial, inverse)
+            magnitude = magnitude_of(strain)
+            keep(i, lanes, EARLY, [strain[n] for n in late_strain] + [magnitude * s for s in strain])
 
     def to_modes(f):
         rows = pl.ds(pl.multiple_of(f * NZ, NZ), NZ)
@@ -346,35 +369,40 @@
             result = dot3((modes_t_h[...], modes_t_l[...]), (field_h[rows, lanes], field_l[rows, lanes]))
             mode_h[place, lanes], mode_l[place, lanes] = split(result)
 
-    loop(FIELDS, to_modes)
-
-    def smooth_group(g):
-        rows = pl.ds(pl.multiple_of(g * 448, 64), 448)
+    def smooth_rows(first, size):
+        rows = pl.ds(pl.multiple_of(first, 64), size)
         for block in range(3):
             lanes = slice(block * 256, (block + 1) * 256)
             result = dot3((mode_h[rows, :], mode_l[rows, :]), (smooth_h[:, lanes], smooth_l[:, lanes]))
-            field_h[rows, lanes], field_l[rows, lanes] = split(result)
-
-    loop(3, smooth_group)
+            smoothed_h[rows, lanes], smoothed_l[rows, lanes] = split(result)
 
     def from_modes(f):
         rows = pl.ds(pl.multiple_of(f * NZ, NZ), NZ)
         place = pl.ds(pl.multiple_of(f * KEPT, KEPT), KEPT)
         for block in range(3):
             lanes = slice(block * 256, (block + 1) * 256)
-            filtered[rows, lanes] = dot3((modes_h[...], modes_l[...]), (field_h[place, lanes], field_l[place, lanes]))
-
-    loop(FIELDS, from_modes)
+            filtered[rows, lanes] = dot3((modes_h[...], modes_l[...]), (smoothed_h[place, lanes], smoothed_l[place, lanes]))
+
+    loop(NZ // 16, early_products)
+    loop(EARLY, to_modes)
+    loop(2, lambda g: smooth_rows(g * 384, 384))
+    loop(EARLY, from_modes)
+    wait_all(rad_z, slope_recv)
+    loop(NZ // 16, late_products)
+    loop(FIELDS - EARLY, lambda f: to_modes(EARLY + f))
+    loop(3, lambda g: smooth_rows(EARLY * KEPT + g * 192, 192))
+    loop(FIELDS - EARLY, lambda f: from_modes(EARLY + f))
 
     def shell_sums(i, sums):
         cross, model_sum = sums
         for block in range(3):
             lanes = slice(block * 256, (block + 1) * 256)
             mean = [filtered[pl.ds(pl.multiple_of(f * NZ + i * 8, 8), 8), lanes] for f in range(FIELDS)]
-            magnitude = magnitude_of(mean[9:15])
+            strain = [mean[place] for place in strain_places]
+            magnitude = magnitude_of(strain)
             for n, (a, b) in enumerate(component_pairs):
                 leonard = mean[3 + n] - mean[a] * mean[b]
-                model = 2.0 * (mean[15 + n] - 4.0 * (magnitude * mean[9 + n]))
+                model = 2.0 * (mean[15 + n] - 4.0 * (magnitude * strain[n]))
                 weighted = model * pair_weights[n]
                 cross = cross + leonard * weighted
                 model_sum = model_sum + model * weighted
@@ -403,7 +431,7 @@
     pltpu.make_async_copy(
         coefficient_own.at[pl.ds(0, 1)], coefficient_all.at[pl.ds(me, 1)], coefficient_recv
     ).start()
-    each_peer(me, share)
+    each_peer(me, core, share)
 
     inverse_row = inverse_rows[pl.ds(core, 1), :]
 
@@ -413,7 +441,8 @@
             [ref[rows, c * HALF : (c + 1) * HALF] for c in range(3)] for ref in (vel_p, rad_p, ang_p, axial_p)
         )
         around = jnp.broadcast_to(inverse_row, (32, HALF))
-        strain, magnitude = strain_of(velocity, radial, angular, axial, around)
+        strain = strain_of(velocity, radial, angular, axial, around)
+        magnitude = magnitude_of(strain)
         carried = velocity[1] * around
         parts = [velocity[0] * radial[c] + carried * angular[c] + velocity[2] * axial[c] for c in range(3)]
         parts[0] = parts[0] - velocity[1] * carried
@@ -443,7 +472,8 @@
 
     for exchange in exchanges:
         exchange.wait_send()
-    wait_sent(vel_t, vel_send)
+    for c in range(3):
+        wait_sent(vel_t.at[:, pl.ds(c * NT, NT)], vel_send.at[c])
     wait_sent(rad_t, slope_send)
     for block in range(3):
         wait_sent(axial_z.at[:, pl.ds(block * NT, NT)], back_send.at[block])
@@ -452,9 +482,31 @@
     pltpu.make_async_copy(scaled, scaled_out, out_sem.at[1]).wait()
 
 
-def finish(conv_ref, scaled_ref, factor_ref, conv_out, stress_out):
-    conv_out[...] = conv_ref[...]
-    stress_out[...] = (scaled_ref[...] * factor_ref[0:1, :]).astype(bf16)
+def finish(
+    conv_ref, scaled_ref, factor_ref, conv_out, stress_out, conv, scaled, stress, conv_in_sem, conv_sem, in_sem, out_sem
+):
+    piece = 6 * NT // PIECES
+
+    def part(i):
+        return pl.ds(i * piece, piece)
+
+    thirds = [pl.ds(c * NT, NT) for c in range(3)]
+    loads = [pltpu.make_async_copy(scaled_ref.at[part(i)], scaled.at[part(i)], in_sem.at[i]) for i in range(PIECES)]
+    moves = [pltpu.make_async_copy(conv_ref.at[c], conv.at[c], conv_in_sem.at[i]) for i, c in enumerate(thirds)]
+    for copy in moves + loads:
+        copy.start()
+    copies = []
+    for i, c in enumerate(thirds):
+        moves[i].wait()
+        copies.append(pltpu.make_async_copy(conv.at[c], conv_out.at[c], conv_sem.at[i]))
+        copies[-1].start()
+    for i in range(PIECES):
+        loads[i].wait()
+        stress[part(i), :] = (scaled[part(i), :] * factor_ref[0:1, :]).astype(bf16)
+        copies.append(pltpu.make_async_copy(stress.at[part(i)], stress_out.at[part(i)], out_sem.at[i]))
+        copies[-1].start()
+    for copy in copies:
+        copy.wait()
 
 
 def shards(coefficients):
@@ -472,7 +524,7 @@
         (plane, f32), (plane, f32), (plane, f32), (plane, bf16), (plane, bf16),
         ([3 * NZ, NT], bf16), ([3 * NZ, NT], bf16), ([3 * NZ, NT], f32),
         ([FIELDS * NZ, NT], bf16), ([FIELDS * NZ, NT], bf16),
-        ([FIELDS * KEPT, NT], bf16), ([FIELDS * KEPT, NT], bf16),
+        ([FIELDS * KEPT, NT], bf16), ([FIELDS * KEPT, NT], bf16), ([FIELDS * KEPT, NT], bf16), ([FIELDS * KEPT, NT], bf16),
         ([FIELDS * NZ, NT], f32), ([6 * NT, HALF], f32), (flat, f32), (plane, f32),
         ([8, 128], f32), ([NZ, 128], f32),
         ([NT, NT], bf16), ([NT, NT], bf16), ([NT, NT], bf16), ([NT, NT], bf16),
@@ -495,25 +547,26 @@
         out_specs=(hbm, hbm, vmem),
         scratch_shapes=[pltpu.VMEM(tuple(shape), kind) for shape, kind in scratch]
         + [semaphore((4,)), semaphore, semaphore((2,)), semaphore((3,)), semaphore((3,))]
-        + [semaphore] * 4
+        + [semaphore((3,)), semaphore((3,)), semaphore, semaphore]
         + [semaphore((3,)), semaphore((3,)), semaphore, semaphore]
         + [pltpu.SemaphoreType.REGULAR] * 2,
         compiler_params=pltpu.CompilerParams(collective_id=0, has_side_effects=True, vmem_limit_bytes=60 << 20),
     )(*operands)
-    steps = 4
     convection, stress = pl.pallas_call(
         finish,
-        grid=(steps,),
         out_shape=(jax.ShapeDtypeStruct((FLAT, HALF), f32), jax.ShapeDtypeStruct((6 * NT, HALF), bf16)),
-        in_specs=[
-            pl.BlockSpec((FLAT // steps, HALF), lambda i: (i, 0)),
-            pl.BlockSpec((6 * NT // steps, HALF), lambda i: (i, 0)),
-            pl.BlockSpec((8, HALF), lambda i: (0, 0)),
+        in_specs=[hbm, hbm, vmem],
+        out_specs=(hbm, hbm),
+        scratch_shapes=[
+            pltpu.VMEM((FLAT, HALF), f32),
+            pltpu.VMEM((6 * NT, HALF), f32),
+            pltpu.VMEM((6 * NT, HALF), bf16),
+            semaphore((3,)),
+            semaphore((3,)),
+            semaphore((PIECES,)),
+            semaphore((PIECES,)),
         ],
-        out_specs=(
-            pl.BlockSpec((FLAT // steps, HALF), lambda i: (i, 0)),
-            pl.BlockSpec((6 * NT // steps, HALF), lambda i: (i, 0)),
-        ),
+        compiler_params=pltpu.CompilerParams(vmem_limit_bytes=60 << 20),
     )(conv, scaled, factor)
     return (convection.reshape(3, 1, NT, HALF), stress.reshape(6, 1, NT, HALF))
 

time: 106 us -> 102 us (0.962)
  Pallas kernels: 105 us -> 101 us
    pallas_call x1, Pallas kernels: 101 us -> 97.6 us  [shards(): pl.pallas_call(kernel, out_shape=(jax.ShapeDtypeStruct((FLAT, HALF), f32)...]
where the time goes in v3:
time: 102 us
  Pallas kernels  101 us (99%)
    pallas_call x1, Pallas kernels, shards(): pl.pallas_call(kernel, out_shape=(jax.ShapeDtypeStruct((FLAT, HALF), f32)...  97.6 us
    pallas_call x1, Pallas kernels, shards(): pl.pallas_call(finish, out_shape=(jax.ShapeDtypeStruct((FLAT, HALF), f32)...  3.78 us

profile of v3, /device:TPU:32, one launch (start us, length us, event | category | flops | bytes accessed | tf_op | source)
XLA Modules:
  0.0 102.0 jit_solution(981093891690214503)
XLA Ops:
  0.6 97.6 %shard_map.158 = (f32[2304,128]{1,0:T(8,128)}, f32[4608,128]{1,0:T(8,128)}, f32[8,128]{1,0:T(8,128)}) custom-call(f32[2304,128]{1,0:T(8,128)} %bitcast.7, bf16[1024,128]{1,0:T(8,128)(2,1)} %constant.28.clone.cheb_h, bf16[1024,128]{1,0:T(8,128)(2,1)} %constant.29.clone.cheb_l, bf16[768,768]{1,0:T(8,128)(2,1)} %constant.30.clone.angle_h_hbm, ...), custom_call_target="tpu_custom_call" | custom-call | tf_op jit(solution)/shard_map/pallas_call | solution.py:542
  98.3 3.8 %shard_map.159 = (f32[2304,128]{1,0:T(8,128)}, bf16[4608,128]{1,0:T(8,128)(2,1)}) custom-call(f32[2304,128]{1,0:T(8,128)} %get-tuple-element.7.conv_ref, f32[4608,128]{1,0:T(8,128)} %get-tuple-element.8.scaled_ref, f32[8,128]{1,0:T(8,128)} %get-tuple-element.9.factor_ref), custom_call_target="tpu_custom_call" | custom-call | tf_op jit(solution)/shard_map/pallas_call | solution.py:555

commit v4 on v3

--- a/solution.py
+++ b/solution.py
@@ -171,12 +171,13 @@
 
 
 def kernel(
-    coef, cheb_h, cheb_l, angle_h_hbm, angle_l_hbm, smooth_h_hbm, smooth_l_hbm, axis_h, axis_l, modes_h, modes_l,
-    modes_t_h, modes_t_l, inverse_rows, inverse_list,
+    coef, cheb_h_hbm, cheb_l_hbm, angle_h_hbm, angle_l_hbm, smooth_h_hbm, smooth_l_hbm, axis_h_hbm, axis_l_hbm,
+    modes_h_hbm, modes_l_hbm, modes_t_h_hbm, modes_t_l_hbm, inverse_rows_hbm, inverse_list_hbm,
     conv_out, scaled_out, factor_out,
     own, other, own_h, own_l, other_h, other_l, vel_t, rad_t, vel_z, rad_z, axial_z, axial_r, vel_p, rad_p, ang_p,
     vel_h, vel_l, vz_h, vz_l, ang_z, field_h, field_l, mode_h, mode_l, smoothed_h, smoothed_l, filtered, scaled, conv, axial_p,
-    coefficient_own, coefficient_all, angle_h, angle_l, smooth_h, smooth_l,
+    coefficient_own, coefficient_all, cheb_h, cheb_l, angle_h, angle_l, smooth_h, smooth_l, axis_h, axis_l, modes_h, modes_l,
+    modes_t_h, modes_t_l, inverse_rows, inverse_list,
     table_sem, in_sem, out_sem, rad_send, rad_recv, vel_send, vel_recv, slope_send, slope_recv, back_send, back_recv,
     coefficient_send, coefficient_recv, in_y, in_x,
 ):
@@ -184,16 +185,6 @@
     core = lax.axis_index("rad")
     partner = 1 - core
 
-    load = pltpu.make_async_copy(coef, own, in_sem)
-    load.start()
-    tables = [
-        pltpu.make_async_copy(source, place, table_sem.at[i])
-        for i, (source, place) in enumerate(
-            ((angle_h_hbm, angle_h), (angle_l_hbm, angle_l), (smooth_h_hbm, smooth_h), (smooth_l_hbm, smooth_l))
-        )
-    ]
-    for table in tables:
-        table.start()
     x, y, z = me // 32, me // 8 % 4, me % 8
     along_z = [x * 32 + y * 8 + (z + k) % 8 for k in range(1, 8)]
     along_y = [x * 32 + (y + k) % 4 * 8 + z for k in range(1, 4)]
@@ -206,6 +197,19 @@
     barrier = pltpu.get_barrier_semaphore()
     pl.semaphore_signal(barrier, 1, device_id={"rad": partner}, device_id_type=MESH)
     greet(barrier, along_z + along_y + along_x)
+    load = pltpu.make_async_copy(coef, own, in_sem)
+    load.start()
+    sources = (
+        cheb_h_hbm, cheb_l_hbm, angle_h_hbm, angle_l_hbm, smooth_h_hbm, smooth_l_hbm, axis_h_hbm, axis_l_hbm,
+        modes_h_hbm, modes_l_hbm, modes_t_h_hbm, modes_t_l_hbm, inverse_rows_hbm, inverse_list_hbm,
+    )
+    places = (
+        cheb_h, cheb_l, angle_h, angle_l, smooth_h, smooth_l, axis_h, axis_l, modes_h, modes_l, modes_t_h, modes_t_l,
+        inverse_rows, inverse_list,
+    )
+    tables = [pltpu.make_async_copy(source, place, table_sem.at[i]) for i, (source, place) in enumerate(zip(sources, places))]
+    for table in tables:
+        table.start()
     pl.semaphore_wait(barrier, 14)
     exchanges = [
         pltpu.make_async_remote_copy(
@@ -253,6 +257,8 @@
             pltpu.make_async_copy(last, last, send).wait()
 
     load.wait()
+    tables[0].wait()
+    tables[1].wait()
 
     def own_part(i):
         rows = pl.ds(pl.multiple_of(i * 256, 256), 256)
@@ -301,7 +307,7 @@
 
         loop(3, plane_part)
 
-    for table in tables:
+    for table in tables[2:]:
         table.wait()
 
     def plane_angle(i):
@@ -330,7 +336,7 @@
         ang_z[:, lanes] = -dot3((vz_h[...], vz_l[...]), (angle_h[:, lanes], angle_l[:, lanes]))
 
     loop(3, shell_angle)
-    inverse = inverse_list[core * HALF + me]
+    inverse = inverse_list[pl.ds(core * HALF + me, 1), :]
 
     def shell_block(i, block):
         rows = pl.ds(pl.multiple_of(i * 16, 16), 16)
@@ -513,7 +519,6 @@
     tables = all_tables()
     hbm = pl.BlockSpec(memory_space=pl.ANY)
     vmem = pl.BlockSpec(memory_space=pltpu.VMEM)
-    smem = pl.BlockSpec(memory_space=pltpu.SMEM)
     flat = [FLAT, HALF]
     shell = [NZ, FLAT]
     plane = [NT, 3 * HALF]
@@ -527,18 +532,19 @@
         ([FIELDS * KEPT, NT], bf16), ([FIELDS * KEPT, NT], bf16), ([FIELDS * KEPT, NT], bf16), ([FIELDS * KEPT, NT], bf16),
         ([FIELDS * NZ, NT], f32), ([6 * NT, HALF], f32), (flat, f32), (plane, f32),
         ([8, 128], f32), ([NZ, 128], f32),
+        ([1024, HALF], bf16), ([1024, HALF], bf16),
         ([NT, NT], bf16), ([NT, NT], bf16), ([NT, NT], bf16), ([NT, NT], bf16),
+        ([NZ, NZ], bf16), ([NZ, NZ], bf16), ([NZ, KEPT], bf16), ([NZ, KEPT], bf16), ([KEPT, NZ], bf16), ([KEPT, NZ], bf16),
+        ([8, HALF], f32), ([NR, 256], f32),
     ]
     inverse = tables["inverse"]
     rows = np.zeros((8, HALF), np.float32)
     rows[:2] = inverse.reshape(2, HALF)
     operands = [coefficients.reshape(FLAT, HALF)]
-    specs = [hbm]
-    for name, spec in (("cheb", vmem), ("angle", hbm), ("smooth", hbm), ("axis", vmem), ("modes", vmem), ("modes_t", vmem)):
+    for name in ("cheb", "angle", "smooth", "axis", "modes", "modes_t"):
         operands += [jnp.asarray(part) for part in tables[name]]
-        specs += [spec, spec]
-    operands += [jnp.asarray(rows), jnp.asarray(inverse)]
-    specs += [vmem, smem]
+    operands += [jnp.asarray(rows), jnp.asarray(np.broadcast_to(inverse[:, None], (NR, 256)).copy())]
+    specs = [hbm] * len(operands)
     conv, scaled, factor = pl.pallas_call(
         kernel,
         out_shape=(jax.ShapeDtypeStruct((FLAT, HALF), f32), jax.ShapeDtypeStruct((6 * NT, HALF), f32),
@@ -546,7 +552,7 @@
         in_specs=specs,
         out_specs=(hbm, hbm, vmem),
         scratch_shapes=[pltpu.VMEM(tuple(shape), kind) for shape, kind in scratch]
-        + [semaphore((4,)), semaphore, semaphore((2,)), semaphore((3,)), semaphore((3,))]
+        + [semaphore((14,)), semaphore, semaphore((2,)), semaphore((3,)), semaphore((3,))]
         + [semaphore((3,)), semaphore((3,)), semaphore, semaphore]
         + [semaphore((3,)), semaphore((3,)), semaphore, semaphore]
         + [pltpu.SemaphoreType.REGULAR] * 2,

time: 102 us -> 101 us (level)
  no operation moved by 1% of the time
where the time goes in v4:
time: 101 us
  Pallas kernels  101 us (100%)
    pallas_call x1, Pallas kernels, shards(): pl.pallas_call(kernel, out_shape=(jax.ShapeDtypeStruct((FLAT, HALF), f32)...  96.9 us
    pallas_call x1, Pallas kernels, shards(): pl.pallas_call(finish, out_shape=(jax.ShapeDtypeStruct((FLAT, HALF), f32)...  3.78 us

profile of v4, /device:TPU:32, one launch (start us, length us, event | category | flops | bytes accessed | tf_op | source)
XLA Modules:
  0.0 101.3 jit_solution(16899705006215455216)
XLA Ops:
  0.6 96.9 %shard_map.158 = (f32[2304,128]{1,0:T(8,128)}, f32[4608,128]{1,0:T(8,128)}, f32[8,128]{1,0:T(8,128)}) custom-call(f32[2304,128]{1,0:T(8,128)} %bitcast.7, bf16[1024,128]{1,0:T(8,128)(2,1)} %constant.28.clone.cheb_h_hbm, bf16[1024,128]{1,0:T(8,128)(2,1)} %constant.29.clone.cheb_l_hbm, bf16[768,768]{1,0:T(8,128)(2,1)} %constant.30.clone.angle_h_hbm, ...), custom_call_target="tpu_custom_call" | custom-call | tf_op jit(solution)/shard_map/pallas_call | solution.py:548
  97.5 3.8 %shard_map.159 = (f32[2304,128]{1,0:T(8,128)}, bf16[4608,128]{1,0:T(8,128)(2,1)}) custom-call(f32[2304,128]{1,0:T(8,128)} %get-tuple-element.7.conv_ref, f32[4608,128]{1,0:T(8,128)} %get-tuple-element.8.scaled_ref, f32[8,128]{1,0:T(8,128)} %get-tuple-element.9.factor_ref), custom_call_target="tpu_custom_call" | custom-call | tf_op jit(solution)/shard_map/pallas_call | solution.py:561

commit v5 on v4

--- a/solution.py
+++ b/solution.py
@@ -260,18 +260,11 @@
     tables[0].wait()
     tables[1].wait()
 
-    def own_part(i):
+    def own_velocity(i):
         rows = pl.ds(pl.multiple_of(i * 256, 256), 256)
         part = split(own[rows, :])
         own_h[rows, :], own_l[rows, :] = part
-        result = dot3(cheb(core, 0, 256), part, True)
-        vel_t[:, rows] = result[:HALF]
-        rad_t[:, rows] = result[HALF:]
-
-    loop(3, own_part)
-    pl.semaphore_wait(in_y, 3)
-    greet(in_x, along_x)
-    loop(6, lambda i: own_part(i + 3))
+        vel_t[:, rows] = dot3(cheb(core, 0, HALF), part, True)
 
     def other_velocity(i):
         rows = pl.ds(pl.multiple_of(i * 256, 256), 256)
@@ -280,17 +273,22 @@
         vel_t[:, rows] += dot3(cheb(partner, 0, HALF), part, True)
 
     for c in range(3):
+        loop(3, lambda i, c=c: own_velocity(i + 3 * c))
+        if c == 0:
+            pl.semaphore_wait(in_y, 3)
+            greet(in_x, along_x)
         exchanges[c].wait_recv()
         loop(3, lambda i, c=c: other_velocity(i + 3 * c))
         if c == 0:
             pl.semaphore_wait(in_x, 3)
         scatter(vel_t, vel_z, vel_send.at[c], vel_recv.at[c], pl.ds(c * NT, NT))
 
-    def other_slope(i):
+    def both_slopes(i):
         rows = pl.ds(pl.multiple_of(i * 256, 256), 256)
-        rad_t[:, rows] += dot3(cheb(partner, HALF, HALF), (other_h[rows, :], other_l[rows, :]), True)
-
-    loop(9, other_slope)
+        result = dot3(cheb(core, HALF, HALF), (own_h[rows, :], own_l[rows, :]), True)
+        rad_t[:, rows] = result + dot3(cheb(partner, HALF, HALF), (other_h[rows, :], other_l[rows, :]), True)
+
+    loop(9, both_slopes)
     scatter(rad_t, rad_z, slope_send, slope_recv)
 
     for c in range(3):

time: 101 us -> 100 us (0.990)
  Pallas kernels: 101 us -> 99.7 us
where the time goes in v5:
time: 100 us
  Pallas kernels  99.7 us (100%)
    pallas_call x1, Pallas kernels, shards(): pl.pallas_call(kernel, out_shape=(jax.ShapeDtypeStruct((FLAT, HALF), f32)...  95.9 us
    pallas_call x1, Pallas kernels, shards(): pl.pallas_call(finish, out_shape=(jax.ShapeDtypeStruct((FLAT, HALF), f32)...  3.78 us

profile of v5, /device:TPU:32, one launch (start us, length us, event | category | flops | bytes accessed | tf_op | source)
XLA Modules:
  0.0 100.4 jit_solution(6211017583280121973)
XLA Ops:
  0.6 95.9 %shard_map.158 = (f32[2304,128]{1,0:T(8,128)}, f32[4608,128]{1,0:T(8,128)}, f32[8,128]{1,0:T(8,128)}) custom-call(f32[2304,128]{1,0:T(8,128)} %bitcast.7, bf16[1024,128]{1,0:T(8,128)(2,1)} %constant.28.clone.cheb_h_hbm, bf16[1024,128]{1,0:T(8,128)(2,1)} %constant.29.clone.cheb_l_hbm, bf16[768,768]{1,0:T(8,128)(2,1)} %constant.30.clone.angle_h_hbm, ...), custom_call_target="tpu_custom_call" | custom-call | tf_op jit(solution)/shard_map/pallas_call | solution.py:546
  96.6 3.8 %shard_map.159 = (f32[2304,128]{1,0:T(8,128)}, bf16[4608,128]{1,0:T(8,128)(2,1)}) custom-call(f32[2304,128]{1,0:T(8,128)} %get-tuple-element.7.conv_ref, f32[4608,128]{1,0:T(8,128)} %get-tuple-element.8.scaled_ref, f32[8,128]{1,0:T(8,128)} %get-tuple-element.9.factor_ref), custom_call_target="tpu_custom_call" | custom-call | tf_op jit(solution)/shard_map/pallas_call | solution.py:559
